TPU v7x, 512 devices: a whole 4x8x8 slice. The times are simulated.
512 devices in a mesh: dp: 32 (over z, x_lo, core), tensor: 16 (over y, x_hi).
Axes of the slice: x: 4 (x_hi: 2, x_lo: 2; x = x_hi * 2 + x_lo), y: 8, z: 8, core: 2. Of those that a mesh axis runs over, the one named last changes fastest.
Arguments:
- queries: bfloat16 [32, 1792, 6144], P('dp', 'tensor'), may hold values from -100 to 100
- keys: bfloat16 [32, 1792, 1024], P('dp', 'tensor'), may hold values from -8 to 8
- values: bfloat16 [32, 1792, 1024], P('dp', 'tensor'), may hold values from -6 to 6
- out_grad: bfloat16 [32, 1792, 6144], P('dp', 'tensor'), may hold values from -6 to 6
- loss_mask: int32 [32, 1792], P('dp', 'tensor'), may hold values from 0 to 1, as said below
Outputs:
- query_grad: bfloat16 [32, 1792, 6144], P('dp', 'tensor')
- key_grad: bfloat16 [32, 1792, 1024], P('dp', 'tensor')
- value_grad: bfloat16 [32, 1792, 1024], P('dp', 'tensor')
Inputs may be any that keep to these rules, and one draw needn't show every extreme that they name: `loss_mask`: the first token of every micro-batch is live.
All inputs are finite; a program needn't handle non-finite values.
Results may differ from a plain program's by a relative error of at most 0.01.
Values may be sent and summed in bfloat16 or wider, within the bound.
A program may use at most 64 MiB of HBM per device.

v0:
```python
import jax
import jax.numpy as jnp
from jax import lax
from jax.sharding import PartitionSpec as P

HD = 128
QH_DEV = 3


def partner_2(value, axis, apart):
    return lax.ppermute(value, axis, [(i, i ^ 1 << apart) for i in range(lax.axis_size(axis))])


def one_head(parts):
    query_head, grad_head, key_part, value_part = parts
    length = query_head.shape[0]
    block = 256
    scale = HD ** (-0.5)
    key_total = jnp.zeros((length, HD), jnp.float32)
    value_total = jnp.zeros((length, HD), jnp.float32)
    query_rows = []
    for number in range(length // block):
        begin_row = number * block
        end_row = begin_row + block
        query_block = query_head[begin_row:end_row]
        grad_block = grad_head[begin_row:end_row]
        key_block = key_part[:end_row]
        value_block = value_part[:end_row]
        scores = jnp.dot(query_block, key_block.T, preferred_element_type=jnp.float32) * scale
        causal = (begin_row + jnp.arange(block))[:, None] >= jnp.arange(end_row)[None, :]
        scores = jnp.where(causal, scores, jnp.float32(-1e30))
        top = jnp.max(scores, axis=-1, keepdims=True)
        probs = jnp.exp(scores - top)
        probs = probs / jnp.sum(probs, axis=-1, keepdims=True)
        probs_b = probs.astype(jnp.bfloat16)
        dprob = jnp.dot(grad_block, value_block.T, preferred_element_type=jnp.float32)
        delta = jnp.sum(probs * dprob, axis=-1, keepdims=True)
        dscore = (probs * (dprob - delta)).astype(jnp.bfloat16)
        query_rows.append(jnp.dot(dscore, key_block, preferred_element_type=jnp.float32) * scale)
        key_total = key_total.at[:end_row].add(
            jnp.dot(dscore.T, query_block, preferred_element_type=jnp.float32) * scale
        )
        value_total = value_total.at[:end_row].add(
            jnp.dot(probs_b.T, grad_block, preferred_element_type=jnp.float32)
        )
    return (jnp.concatenate(query_rows, axis=0), key_total, value_total)


def body(queries, keys, values, out_grad, loss_mask):
    ways = lax.axis_size("tensor")
    tok = queries.shape[1]
    whole = tok * ways
    count = lax.psum(jnp.sum(loss_mask.astype(jnp.float32)), ("dp", "tensor"))
    factor = jnp.float32(lax.axis_size("dp") * whole) / count
    masked = out_grad[0] * loss_mask[0][:, None].astype(jnp.bfloat16)
    key_all, value_all = (
        lax.all_gather(keys[0], "tensor", axis=0, tiled=True),
        lax.all_gather(values[0], "tensor", axis=0, tiled=True),
    )
    start = lax.axis_index("tensor") // 2 * HD
    key_head = lax.dynamic_slice_in_dim(key_all, start, HD, 1)
    value_head = lax.dynamic_slice_in_dim(value_all, start, HD, 1)
    query_four = queries[0].reshape(tok, ways, QH_DEV, HD)
    grad_four = masked.reshape(tok, ways, QH_DEV, HD)
    query_piece = lax.all_to_all(query_four, "tensor", split_axis=1, concat_axis=0, tiled=True)
    grad_piece = lax.all_to_all(grad_four, "tensor", split_axis=1, concat_axis=0, tiled=True)
    length = query_piece.shape[0]
    width = query_piece.shape[2]
    query_heads = jnp.transpose(query_piece.reshape(length, width, HD), (1, 0, 2))
    grad_heads = jnp.transpose(grad_piece.reshape(length, width, HD), (1, 0, 2))
    key_rep = jnp.broadcast_to(key_head[None], (width, length, HD))
    value_rep = jnp.broadcast_to(value_head[None], (width, length, HD))
    results = lax.map(one_head, (query_heads, grad_heads, key_rep, value_rep))
    query_terms, key_terms, value_terms = tuple(
        (jnp.transpose(item, (1, 0, 2)).reshape(length, 1, width, HD) for item in results)
    )
    query_rounded = (query_terms * factor).astype(jnp.bfloat16)
    query_back = lax.all_to_all(query_rounded, "tensor", split_axis=0, concat_axis=1, tiled=True)
    query_grad = query_back.reshape(1, tok, -1)
    key_part = (jnp.sum(key_terms, axis=(1, 2)) * factor).astype(jnp.bfloat16)
    value_part = (jnp.sum(value_terms, axis=(1, 2)) * factor).astype(jnp.bfloat16)
    even_side = lax.axis_index("tensor") % 2 == 0
    outgoing = jnp.where(even_side, value_part, key_part)
    keeping = jnp.where(even_side, key_part, value_part)
    partner = partner_2(outgoing, "tensor", 0)
    summed = (keeping.astype(jnp.float32) + partner.astype(jnp.float32)).astype(jnp.bfloat16)
    back = lax.all_to_all(
        summed.reshape(ways, tok, 1, HD), "tensor", split_axis=0, concat_axis=2, tiled=True
    )
    sorted_back = back[0].reshape(tok, ways // 2, 2, HD)
    key_grad = sorted_back[:, :, 0, :].reshape(1, tok, -1)
    value_grad = sorted_back[:, :, 1, :].reshape(1, tok, -1)
    return (query_grad, key_grad, value_grad)


def solution(mesh):
    return jax.shard_map(
        body,
        mesh=mesh,
        in_specs=(
            P("dp", "tensor", None),
            P("dp", "tensor", None),
            P("dp", "tensor", None),
            P("dp", "tensor", None),
            P("dp", "tensor"),
        ),
        out_specs=(P("dp", "tensor", None), P("dp", "tensor", None), P("dp", "tensor", None)),
        check_vma=False,
    )
```

profile of v0, /device:TPU:24, one launch (start us, length us, event | category | flops | bytes accessed | tf_op | source)
XLA Modules:
  0.0 410.5 jit_solution(14864483071323881137)
XLA Ops:
  7.2 0.7 all-gather.5.cloned.1.call-update
  7.9 0.7 all-gather.7.cloned.1.call-update
  8.6 1.9 copy.34
  10.5 1.5 copy.35
  12.1 9.9 %all-to-all-start = ((bf16[112,16,3,128]{3,0,2,1:T(8,128)(2,1)}), bf16[112,16,3,128]{3,0,2,1:T(8,128)(2,1)}, u32[]{:S(2)}, u32[]{:S(2)}) async-start(bf16[112,16,3,128]{3,0,2,1:T(8,128)(2,1)} %copy.35), calls=%async_computation | async-start | bytes 2752512 | tf_op jit(solution)/shard_map/all_to_all | solution.py:65
  22.0 0.9 copy.37
  23.1 1.6 copy.38
  24.6 38.8 %all-to-all-done = bf16[112,16,3,128]{3,0,2,1:T(8,128)(2,1)} async-done(((bf16[112,16,3,128]{3,0,2,1:T(8,128)(2,1)}), bf16[112,16,3,128]{3,0,2,1:T(8,128)(2,1)}, u32[]{:S(2)}, u32[]{:S(2)}) %all-to-all-start) | async-done | bytes 1376288 | tf_op jit(solution)/shard_map/all_to_all | solution.py:65
  63.5 5.8 %all-to-all-start.1 = ((bf16[112,16,3,128]{3,0,2,1:T(8,128)(2,1)}), bf16[112,16,3,128]{3,0,2,1:T(8,128)(2,1)S(1)}, u32[]{:S(2)}, u32[]{:S(2)}) async-start(bf16[112,16,3,128]{3,0,2,1:T(8,128)(2,1)} %copy.38), calls=%async_computation.1 | async-start | bytes 2752512 | tf_op jit(solution)/shard_map/all_to_all | solution.py:66
  69.8 134.2 %psum.7 = f32[]{:T(128)} all-reduce(f32[]{:T(128)} %convert_reduce_fusion), channel_id=1, replica_groups=mesh['dp'=32,'tensor'=16] {'dp','tensor'}, use_global_device_ids=true, to_apply=%region_24.25 | all-reduce | flops 1 | bytes 8 | tf_op jit(solution)/shard_map/psum | solution.py:53
  204.7 1.4 copy.36
  206.2 1.2 copy.39
  207.3 1.0 dynamic-slice_bitcast_fusion.73
  208.4 34.0 %all-gather.7.cloned.1.call-done = bf16[1,1792,1024]{2,1,0:T(8,128)(2,1)} async-done(((bf16[1,112,1024]{2,1,0:T(8,128)(2,1)}), bf16[1,1792,1024]{2,1,0:T(8,128)(2,1)}) %all-gather.7.cloned.1.call-update) | async-done | bytes 3670032 | tf_op jit(solution)/shard_map/all_gather | solution.py:58
  242.4 1.0 dynamic-slice_bitcast_fusion.72
  243.5 1.2 broadcast_in_dim.126
  244.8 71.0 %while.33 = (s32[]{:T(128)}, f32[3,1792,128]{2,1,0:T(8,128)}, f32[3,1792,128]{2,1,0:T(8,128)}, f32[3,1792,128]{2,1,0:T(8,128)}, bf16[3,1792,128]{2,1,0:T(8,128)(...) while((s32[]{:T(128)}, f32[3,1792,128]{2,1,0:T(8,128)}, ...), condition=%wide.region_22.23_spmd, body=%wide.region_0.22_spmd.sunk | while | flops 2384752896 | bytes 99860888 | solution.py:73
  245.3 1.1 fusion.239
  246.4 1.1 multiply_reduce_fusion.14
  263.0 1.6 fusion.245
  264.6 0.6 multiply_reduce_fusion.20
  266.2 1.4 fusion.238
  267.6 1.0 bitcast_dynamic-update-slice_fusion.2
  269.0 1.1 fusion.239
  270.1 1.1 multiply_reduce_fusion.14
  286.6 1.6 fusion.245
  289.8 1.4 fusion.238
  291.2 1.0 bitcast_dynamic-update-slice_fusion.2
  292.6 1.1 fusion.239
  293.7 1.1 multiply_reduce_fusion.14
  310.3 1.6 fusion.245
  311.8 0.6 multiply_reduce_fusion.20
  313.4 1.4 fusion.238
  314.8 1.0 bitcast_dynamic-update-slice_fusion.2
  315.8 2.0 reduce_sum.211
  317.8 2.0 reduce_sum.210
  320.0 2.5 collective-permute-start
  322.5 9.4 %collective-permute-done = bf16[1792,128]{1,0:T(8,128)(2,1)S(1)} collective-permute-done((bf16[1792,128]{1,0:T(8,128)(2,1)S(1)}, bf16[1792,128]{1,0:T(8,128)(2,1)S(1)}, u32[]{:S(2)}, u32[]{:S(2)}) %collective-permute-start) | collective-permute-done | bytes 458784 | tf_op jit(solution)/shard_map/ppermute | solution.py:11
  331.9 0.9 add_convert_fusion
  332.8 6.1 %all-to-all-start.3 = ((bf16[16,112,1,128]{3,1,2,0:T(8,128)(2,1)}), bf16[16,112,1,128]{3,1,2,0:T(8,128)(2,1)S(1)}, u32[]{:S(2)}, u32[]{:S(2)}) async-start(bf16[16,112,1,128]{3,1,2,0:T(8,128)(2,1)} %bitcast.49), calls=%async_computation.3 | async-start | bytes 917504 | tf_op jit(solution)/shard_map/all_to_all | solution.py:87
  338.9 2.0 fusion.111
  340.9 9.5 %copy.40 = bf16[1792,1,3,128]{3,2,1,0:T(4,128)(2,1)} copy(bf16[1792,1,3,128]{3,0,2,1:T(8,128)(2,1)S(1)} %fusion.111) | data formatting | bytes 2752512 | tf_op jit(solution)/shard_map/convert_element_type | solution.py:77
  350.9 9.1 %all-to-all-start.2 = ((bf16[1792,1,3,128]{3,2,1,0:T(4,128)(2,1)}), bf16[1792,1,3,128]{3,2,1,0:T(4,128)(2,1)S(1)}, u32[]{:S(2)}, u32[]{:S(2)}) async-start(bf16[1792,1,3,128]{3,2,1,0:T(4,128)(2,1)} %copy.40), calls=%async_computation.2 | async-start | bytes 3670016 | tf_op jit(solution)/shard_map/all_to_all | solution.py:78
  360.1 0.8 reshape_squeeze.15
  361.0 0.8 reshape_squeeze.14
  361.8 39.3 %all-to-all-done.2 = bf16[1792,1,3,128]{3,2,1,0:T(4,128)(2,1)S(1)} async-done(((bf16[1792,1,3,128]{3,2,1,0:T(4,128)(2,1)}), bf16[1792,1,3,128]{3,2,1,0:T(4,128)(2,1)S(1)}, u32[]{:S(2)}, u32[]{:S(2)}) %all-to-all-start.2) | async-done | bytes 1376288 | tf_op jit(solution)/shard_map/all_to_all | solution.py:78
  401.0 1.1 copy.41
  402.2 1.5 copy.44
  (189 shorter events, 52.1 us)
Async XLA Ops:
  7.2 200.2 %all-gather.5.cloned.1.call-start = ((), (), s32[]{:S(2)}) async-start(), calls=%async_computation.4 | async-start | bytes 3899392 | tf_op jit(solution)/shard_map/all_gather | solution.py:57
  7.9 234.5 %all-gather.7.cloned.1.call-start = ((), (), s32[]{:S(2)}) async-start(), calls=%async_computation.5 | async-start | bytes 3899392 | tf_op jit(solution)/shard_map/all_gather | solution.py:58
  12.1 9.9 %copy-start = (bf16[1,112,6144]{2,1,0:T(8,128)(2,1)S(1)}, bf16[1,112,6144]{2,1,0:T(8,128)(2,1)}, u32[]{:S(2)}) copy-start(bf16[1,112,6144]{2,1,0:T(8,128)(2,1)} %param.42) | copy-start | bytes 4128772
  12.1 51.4 %all-to-all-start = ((bf16[112,16,3,128]{3,0,2,1:T(8,128)(2,1)}), bf16[112,16,3,128]{3,0,2,1:T(8,128)(2,1)}, u32[]{:S(2)}, u32[]{:S(2)}) async-start(bf16[112,16,3,128]{3,0,2,1:T(8,128)(2,1)} %copy.35), calls=%async_computation | async-start | bytes 2752512 | tf_op jit(solution)/shard_map/all_to_all | solution.py:65
  22.0 0.9 copy-start.3
  63.5 142.7 %all-to-all-start.1 = ((bf16[112,16,3,128]{3,0,2,1:T(8,128)(2,1)}), bf16[112,16,3,128]{3,0,2,1:T(8,128)(2,1)S(1)}, u32[]{:S(2)}, u32[]{:S(2)}) async-start(bf16[112,16,3,128]{3,0,2,1:T(8,128)(2,1)} %copy.38), calls=%async_computation.1 | async-start | bytes 2752512 | tf_op jit(solution)/shard_map/all_to_all | solution.py:66
  245.0 1.4 copy-start.1
  247.5 1.3 copy-start.2
  268.6 1.4 copy-start.1
  271.1 1.3 copy-start.2
  292.2 1.4 copy-start.1
  294.7 1.3 copy-start.2
  320.0 11.9 %collective-permute-start = (bf16[1792,128]{1,0:T(8,128)(2,1)S(1)}, bf16[1792,128]{1,0:T(8,128)(2,1)S(1)}, u32[]{:S(2)}, u32[]{:S(2)}) collective-permute-start(bf16[1792,128]{1,0:T(8,128)(2,1)S(1)} %broadcast_select_fusion), channel_id=1, source_target_pairs={{0,1},{1,0},{2,3},{3,2},{4,5},{5,4},{6,7},{7,6},{8,9},{9,8},{10,11... | collective-permute-start | bytes 1376264 | tf_op jit(solution)/shard_map/ppermute | solution.py:11
  332.8 18.1 %all-to-all-start.3 = ((bf16[16,112,1,128]{3,1,2,0:T(8,128)(2,1)}), bf16[16,112,1,128]{3,1,2,0:T(8,128)(2,1)S(1)}, u32[]{:S(2)}, u32[]{:S(2)}) async-start(bf16[16,112,1,128]{3,1,2,0:T(8,128)(2,1)} %bitcast.49), calls=%async_computation.3 | async-start | bytes 917504 | tf_op jit(solution)/shard_map/all_to_all | solution.py:87
  350.9 50.1 %all-to-all-start.2 = ((bf16[1792,1,3,128]{3,2,1,0:T(4,128)(2,1)}), bf16[1792,1,3,128]{3,2,1,0:T(4,128)(2,1)S(1)}, u32[]{:S(2)}, u32[]{:S(2)}) async-start(bf16[1792,1,3,128]{3,2,1,0:T(4,128)(2,1)} %copy.40), calls=%async_computation.2 | async-start | bytes 3670016 | tf_op jit(solution)/shard_map/all_to_all | solution.py:78
Sparse Core Ops, SparseCore 0:
  11.2 128.8 all-gather.4
  143.2 99.1 all-gather.6
where the time goes:
time: 412 us; the launch traced here: 411 us
  blocking collectives  134 us (33%)
  waiting for transfers between devices  124 us (30%)
  matrix products  52.1 us (13%)
  starting transfers between devices  33.4 us (8%)
  local copies, waits for them, and re-layouts  30.7 us (7%)
  other arithmetic  20.8 us (5%)
  between operations  14.9 us (4%)
    psum x1, blocking collectives, body(): count = lax.psum(jnp.sum(loss_mask.astype(jnp.float32)), ('dp', 'tensor'))  134 us
    all_to_all x1, waiting for transfers between devices, body(): lax.all_to_all(query_rounded, 'tensor', split_axis=0, concat_axis=1, tile...  39.3 us
    all_to_all x1, waiting for transfers between devices, body(): lax.all_to_all(query_four, 'tensor', split_axis=1, concat_axis=0, tiled=T...  38.8 us
    all_gather x1, waiting for transfers between devices, body(): lax.all_gather(values[0], 'tensor', axis=0, tiled=True)  34 us
    dot_general x21, matrix products, one_head(): jnp.dot(probs_b.T, grad_block, preferred_element_type=jnp.float32)  15.7 us
    dot_general x21, matrix products, one_head(): jnp.dot(grad_block, value_block.T, preferred_element_type=jnp.float32)  11.4 us
    dot_general x21, matrix products, one_head(): jnp.dot(dscore.T, query_block, preferred_element_type=jnp.float32) * scale  10.2 us
    all_to_all x1, starting transfers between devices, body(): lax.all_to_all(query_four, 'tensor', split_axis=1, concat_axis=0, tiled=T...  9.93 us
  transfers between devices with their start and end apart: 7, of which 5 were waited for; matrix products, arithmetic and copies ran while one was open for 6% of the time, Pallas kernels for 0%

commit v1 on v0

v1 whole, which is shorter than its diff:
```python
import jax
import jax.numpy as jnp
from jax import lax
from jax.experimental import pallas as pl
from jax.experimental.pallas import tpu as pltpu
from jax.sharding import PartitionSpec as P

HD = 128
KVH = 8
GROUP = 6
KVD = KVH // 2
RING = 8
UP = 4
DOWN = 3
SCALE = HD**-0.5
SCALE2 = SCALE * 1.4426950408889634
NT = (((1,), (1,)), ((), ()))
TN = (((0,), (0,)), ((), ()))
MESH = pl.DeviceIdType.MESH
f32 = jnp.float32
bf16 = jnp.bfloat16


def fold8(x):
    return x.reshape(x.shape[0] // 8, 8, x.shape[1])


def make_kernel(tok, dp_size, ways, block):
    rows2 = GROUP * tok
    rows = 2 * rows2
    pair = 2 * tok
    length = ways * tok
    blocks = length // block
    chunks = [(i, min(256, rows - i)) for i in range(0, rows, 256)]
    dp_bits = dp_size.bit_length() - 1
    t_bits = ways.bit_length() - 1

    def kernel(
        q_ref, k_ref, v_ref, g_ref, mask_ref, dq_ref, dk_ref, dv_ref,
        qg, kv, qg_out, kv_out, sbuf, pbuf, ebuf, dsb, dqt, qn, gn, stat, rowpos,
        part, rs_out, rs_in, dq_out, dq_in, dkv_out, dkv_in, cnt_out, cnt_in,
        x_send, x_recv, ag_send, ag_recv, rs_send, rs_recv, cnt_send, cnt_recv,
    ):
        me_dp = lax.axis_index("dp")
        me = lax.axis_index("tensor")
        side = lax.rem(me, 2)
        y = me // 2

        def flip(index, bit):
            step = 1 << bit
            return index + step * (1 - 2 * lax.rem(index // step, 2))

        other = (me_dp, flip(me, 0))
        above = (me_dp, lax.rem(me + 2, ways))
        below = (me_dp, lax.rem(me + ways - 2, ways))
        doubling = [(me_dp, flip(me, bit)) for bit in range(t_bits)] + [
            (flip(me_dp, bit), me) for bit in range(dp_bits)
        ]
        peers = [other, above, below] + doubling[2:]

        @pl.when(y < RING - 1)
        def _():
            after = pl.ds(pl.multiple_of((y + 1) * pair, 16), pair)
            for h in range(KVD):
                kv[h, :, after, :] = jnp.zeros((2, pair, HD), bf16)

        barrier = pltpu.get_barrier_semaphore()
        for peer in peers:
            pl.semaphore_signal(barrier, inc=1, device_id=peer, device_id_type=MESH)

        def remote(src, dst, send, recv, device):
            return pltpu.make_async_remote_copy(
                src_ref=src, dst_ref=dst, send_sem=send, recv_sem=recv,
                device_id=device, device_id_type=MESH,
            )

        mask_row = mask_ref[...].astype(f32)
        eye = lax.broadcasted_iota(jnp.int32, (tok, tok), 0) == lax.broadcasted_iota(
            jnp.int32, (tok, tok), 1
        )
        mask_col = jnp.sum(jnp.where(eye, mask_row, 0.0), axis=1, keepdims=True)
        mask_tile = jnp.broadcast_to(mask_col, (tok, HD)).astype(bf16)
        cnt_out[0] = jnp.full((8, 128), jnp.sum(mask_row, keepdims=True)[0:1, 0:1], f32)

        own_rows = pl.multiple_of(side * rows2, 16)
        own_tok = pl.multiple_of(y * pair + side * tok, 16)

        def stage(h, _):
            for p in range(GROUP):
                at = pl.ds(p * tok, tok)
                mine = pl.ds(pl.multiple_of(((side * KVD + h) * GROUP + p) * HD, HD), HD)
                theirs = pl.ds(pl.multiple_of((((1 - side) * KVD + h) * GROUP + p) * HD, HD), HD)
                keep = pl.ds(pl.multiple_of(own_rows + p * tok, 16), tok)
                qg[h, 0, keep, :] = q_ref[:, mine]
                qg[h, 1, keep, :] = g_ref[:, mine] * mask_tile
                qg_out[h, 0, at, :] = q_ref[:, theirs]
                qg_out[h, 1, at, :] = g_ref[:, theirs] * mask_tile
            mine = pl.ds(pl.multiple_of((side * KVD + h) * HD, HD), HD)
            theirs = pl.ds(pl.multiple_of(((1 - side) * KVD + h) * HD, HD), HD)
            kv[h, 0, pl.ds(own_tok, tok), :] = k_ref[:, mine]
            kv[h, 1, pl.ds(own_tok, tok), :] = v_ref[:, mine]
            kv_out[h, 0] = k_ref[:, theirs]
            kv_out[h, 1] = v_ref[:, theirs]
            return 0

        lax.fori_loop(0, KVD, stage, 0)
        index = lax.broadcasted_iota(jnp.int32, (8, rows), 1)
        place = index
        for step in range(1, 2 * GROUP):
            place = place - jnp.where(index >= step * tok, tok, 0)
        rowpos[...] = place + jnp.where(index >= rows2, tok, 0)

        pl.semaphore_wait(barrier, len(peers))

        def x_copy(kind, h):
            src, dst = {
                0: lambda: (kv_out.at[h], kv.at[h, :, pl.ds(own_tok, tok), :]),
                1: lambda: (qg_out.at[h], qg.at[h, :, pl.ds(own_rows, rows2), :]),
                2: lambda: (dq_out.at[h], dq_in.at[h]),
                3: lambda: (dkv_out.at[h], dkv_in.at[h]),
            }[kind]()
            return remote(src, dst, x_send.at[kind, h], x_recv.at[kind, h], other)

        def ag_copy(h, s, up):
            j = y - s if up else lax.rem(y + s, RING)
            span = pl.ds(pl.multiple_of(jnp.maximum(j, 0) * pair, 16), pair)
            place = kv.at[h, :, span, :]
            slot = s if up else UP + s
            return remote(
                place, place, ag_send.at[h, slot], ag_recv.at[h, slot], above if up else below
            )

        def ag_send_when(s, up):
            if up:
                return jnp.logical_and(y < RING - 1, y >= s)
            return lax.rem(y + s, RING) < DOWN

        def ag_recv_when(s, up):
            if up:
                return y >= s + 1
            return lax.rem(y + 1 + s, RING) < DOWN

        def ag_start(h, s):
            for up in (True, False):
                if s < (UP if up else DOWN):
                    pl.when(ag_send_when(s, up))(lambda up=up: ag_copy(h, s, up).start())

        def ag_wait(h, s):
            for up in (True, False):
                if s < (UP if up else DOWN):
                    pl.when(ag_recv_when(s, up))(lambda up=up: ag_copy(h, s, up).wait_recv())

        def rs_copy(h, s, down):
            slot = s if down else UP + s
            return remote(
                rs_out.at[h, slot], rs_in.at[h, slot], rs_send.at[h, slot], rs_recv.at[h, slot],
                below if down else above,
            )

        def rs_block(s, down):
            return y - UP + s if down else lax.rem(y + DOWN - s, RING)

        def rs_send_when(s, down):
            if down:
                return y >= UP - s
            return lax.rem(y + DOWN - s, RING) < DOWN

        def rs_recv_when(s, down):
            if down:
                return jnp.logical_and(y < RING - 1, y >= UP - 1 - s)
            return lax.rem(y + DOWN - 1 - s, RING) < DOWN

        def rs_take(h, s, down):
            pl.when(rs_recv_when(s, down))(lambda: rs_copy(h, s, down).wait_recv())

        def part_scaled(h, j):
            span = pl.ds(pl.multiple_of(jnp.maximum(j, 0) * pair, 16), pair)
            slot = lax.rem(h, 2)
            return [part[slot, i, span, :] for i in range(2)]

        def rs_start(h, s):
            for down in (True, False):
                if s >= (UP if down else DOWN):
                    continue
                if s > 0:
                    rs_take(h, s - 1, down)
                slot = s if down else UP + s
                j = rs_block(s, down)
                here = rs_send_when(s, down)
                if down:
                    first = jnp.logical_or(y == RING - 1, s == 0)
                    cases = [(True, False, first), (True, True, jnp.logical_not(first))]
                else:
                    owns = y > j
                    cases = [(True, s > 0, owns)] + (
                        [(False, True, jnp.logical_not(owns))] if s > 0 else []
                    )
                for mine, came, when in cases:
                    if down and came and s == 0:
                        continue

                    def fill(mine=mine, came=came, slot=slot, j=j, down=down):
                        values = part_scaled(h, j) if mine else None
                        for i in range(2):
                            if mine and came:
                                total = values[i] + rs_in[h, slot - 1, i].astype(f32)
                                rs_out[h, slot, i] = total.astype(bf16)
                            elif mine:
                                rs_out[h, slot, i] = values[i].astype(bf16)
                            else:
                                rs_out[h, slot, i] = rs_in[h, slot - 1, i]
                        rs_copy(h, s, down).start()

                    pl.when(jnp.logical_and(here, when))(fill)

        def rs_finish(h):
            rs_take(h, UP - 1, True)
            rs_take(h, DOWN - 1, False)
            slot = lax.rem(h, 2)
            mine_at = pl.ds(own_tok, tok)
            theirs_at = pl.ds(pl.multiple_of(y * pair + (1 - side) * tok, 16), tok)
            mine_in = pl.ds(pl.multiple_of(side * tok, 16), tok)
            theirs_in = pl.ds(pl.multiple_of((1 - side) * tok, 16), tok)
            columns = pl.ds(pl.multiple_of((side * KVD + h) * HD, HD), HD)
            from_above = y < RING - 1
            from_below = y < DOWN

            def total(i, at, within, above_too, below_too):
                value = part[slot, i, at, :]
                if above_too:
                    value = value + rs_in[h, UP - 1, i, within, :].astype(f32)
                if below_too:
                    value = value + rs_in[h, UP + DOWN - 1, i, within, :].astype(f32)
                return value.astype(bf16)

            for above_too, below_too, when in (
                (True, True, from_below),
                (True, False, jnp.logical_and(from_above, jnp.logical_not(from_below))),
                (False, False, jnp.logical_not(from_above)),
            ):

                def fill(above_too=above_too, below_too=below_too):
                    for i, ref in ((0, dk_ref), (1, dv_ref)):
                        dkv_out[h, i] = total(i, theirs_at, theirs_in, above_too, below_too)
                        ref[:, columns] = total(i, mine_at, mine_in, above_too, below_too)

                pl.when(when)(fill)
            x_copy(3, h).start()

        def count_copy(n):
            return remote(
                cnt_out.at[n], cnt_in.at[n], cnt_send.at[n], cnt_recv.at[n], doubling[n]
            )

        count_left = list(range(len(doubling)))

        def count_rounds(number):
            for _ in range(number):
                if not count_left:
                    return
                n = count_left.pop(0)
                copy = count_copy(n)
                copy.start()
                copy.wait_recv()
                cnt_out[n + 1] = cnt_out[n] + cnt_in[n]

        x_copy(0, 0).start()
        x_copy(1, 0).start()
        for h in range(1, KVD):
            x_copy(0, h).start()
        count_rounds(1)
        x_copy(0, 0).wait_recv()
        ag_start(0, 0)
        for s in range(1, UP):
            count_rounds(2)
            ag_wait(0, s - 1)
            ag_start(0, s)
        count_rounds(len(doubling))
        ag_wait(0, UP - 1)
        count = cnt_out[len(doubling)]
        factor = f32(dp_size * length) / count[0:1, :]

        full_blocks = (pair * y + 1) // block
        all_blocks = jnp.minimum(blocks, (pair * (y + 1) + block - 1) // block)

        def one_head(h, _):
            more = h + 1 < KVD
            before = h > 0
            x_copy(1, h).wait_recv()

            @pl.when(more)
            def _():
                x_copy(1, h + 1).start()
                x_copy(0, h + 1).wait_recv()
                ag_start(h + 1, 0)

            def between(s):
                pl.when(more)(lambda: (ag_wait(h + 1, s - 1), ag_start(h + 1, s))[0])
                pl.when(before)(lambda: rs_start(h - 1, s))

            stat[0] = jnp.full((8, rows), -1e30, f32)

            def scores(masked):
                def step(b, _):
                    at = pl.ds(pl.multiple_of(b * block, block), block)
                    key_block = kv[h, 0, at, :]
                    value_block = kv[h, 1, at, :]
                    for c0, cw in chunks:
                        cs = pl.ds(c0, cw)
                        s = lax.dot_general(
                            key_block, qg[h, 0, cs, :], NT, preferred_element_type=f32
                        )
                        if masked:
                            key_at = (
                                b * block - pair * y
                                + lax.broadcasted_iota(jnp.int32, (block, cw), 0)
                            )
                            s = jnp.where(key_at <= rowpos[0:1, cs], s, -1e30)
                        sbuf[at, cs] = s
                        stat[0, :, cs] = jnp.maximum(stat[0, :, cs], jnp.max(fold8(s), axis=0))
                        pbuf[at, cs] = lax.dot_general(
                            value_block, qg[h, 1, cs, :], NT, preferred_element_type=f32
                        )
                    return 0

                return step

            lax.fori_loop(0, full_blocks, scores(False), 0)
            lax.fori_loop(full_blocks, all_blocks, scores(True), 0)
            between(1)
            top = jnp.max(stat[0], axis=0, keepdims=True) * SCALE2
            stat[0] = jnp.broadcast_to(top, (8, rows))
            stat[1] = jnp.zeros((8, rows), f32)
            stat[2] = jnp.zeros((8, rows), f32)

            def weights(b, _):
                at = pl.ds(pl.multiple_of(b * block, block), block)
                for c0, cw in chunks:
                    cs = pl.ds(c0, cw)
                    e = jnp.exp2(sbuf[at, cs] * SCALE2 - stat[0, 0:1, cs])
                    ebuf[at, cs] = e.astype(bf16)
                    stat[1, :, cs] += jnp.sum(fold8(e), axis=0)
                    stat[2, :, cs] += jnp.sum(fold8(e * pbuf[at, cs]), axis=0)
                return 0

            lax.fori_loop(0, all_blocks, weights, 0)
            between(2)
            inverse = 1.0 / jnp.sum(stat[1], axis=0, keepdims=True)
            delta = jnp.sum(stat[2], axis=0, keepdims=True) * inverse
            stat[3] = jnp.broadcast_to(delta, (8, rows))
            inverse_column = jnp.transpose(jnp.broadcast_to(inverse, (8, rows)))[:, 0:1]
            qn[...] = (qg[h, 0].astype(f32) * inverse_column).astype(bf16)
            gn[...] = (qg[h, 1].astype(f32) * inverse_column).astype(bf16)
            dqt[...] = jnp.zeros((HD, rows), f32)
            slot = lax.rem(h, 2)

            def grads(b, _):
                at = pl.ds(pl.multiple_of(b * block, block), block)
                key_block = kv[h, 0, at, :]
                for c0, cw in chunks:
                    cs = pl.ds(c0, cw)
                    ds = ebuf[at, cs] * (pbuf[at, cs] - stat[3, 0:1, cs]).astype(bf16)
                    dsb[:, cs] = ds
                    dqt[:, cs] += lax.dot_general(key_block, ds, TN, preferred_element_type=f32)
                part[slot, 1, at, :] = factor * jnp.dot(
                    ebuf[at, :], gn[...], preferred_element_type=f32
                )
                part[slot, 0, at, :] = (factor * SCALE) * jnp.dot(
                    dsb[...], qn[...], preferred_element_type=f32
                )
                return 0

            lax.fori_loop(0, all_blocks, grads, 0)
            between(3)
            rs_start(h, 0)
            stat[0] = jnp.broadcast_to(inverse * (factor[:, 0:1] * SCALE), (8, rows))
            dqt[...] = dqt[...] * stat[0, 0:1, :]
            dq_rows = jnp.transpose(dqt[...]).astype(bf16)

            def hand_out(mine, theirs):
                dq_out[h] = theirs
                for p in range(GROUP):
                    column = pl.multiple_of(((side * KVD + h) * GROUP + p) * HD, HD)
                    dq_ref[:, pl.ds(column, HD)] = mine[p * tok : (p + 1) * tok]

            pl.when(side == 0)(lambda: hand_out(dq_rows[:rows2], dq_rows[rows2:]))
            pl.when(side == 1)(lambda: hand_out(dq_rows[rows2:], dq_rows[:rows2]))
            x_copy(2, h).start()
            pl.when(more)(lambda: ag_wait(h + 1, UP - 1))
            pl.when(before)(lambda: rs_finish(h - 1))
            return 0

        lax.fori_loop(0, KVD, one_head, 0)
        last = KVD - 1
        for s in range(1, UP):
            rs_start(last, s)
        rs_finish(last)

        def collect(h, _):
            x_copy(2, h).wait_recv()
            for p in range(GROUP):
                column = pl.multiple_of((((1 - side) * KVD + h) * GROUP + p) * HD, HD)
                dq_ref[:, pl.ds(column, HD)] = dq_in[h, p * tok : (p + 1) * tok, :]
            x_copy(3, h).wait_recv()
            columns = pl.ds(pl.multiple_of(((1 - side) * KVD + h) * HD, HD), HD)
            dk_ref[:, columns] = dkv_in[h, 0]
            dv_ref[:, columns] = dkv_in[h, 1]
            for kind in range(4):
                x_copy(kind, h).wait_send()
            for s in range(UP):
                for way in (True, False):
                    if s < (UP if way else DOWN):
                        pl.when(ag_send_when(s, way))(
                            lambda s=s, way=way: ag_copy(h, s, way).wait_send()
                        )
                        pl.when(rs_send_when(s, way))(
                            lambda s=s, way=way: rs_copy(h, s, way).wait_send()
                        )
            return 0

        lax.fori_loop(0, KVD, collect, 0)
        for n in range(len(doubling)):
            count_copy(n).wait_send()

    steps = UP + DOWN
    rounds = t_bits + dp_bits
    dma = pltpu.SemaphoreType.DMA
    scratch = [
        pltpu.VMEM((KVD, 2, rows, HD), bf16),
        pltpu.VMEM((KVD, 2, length, HD), bf16),
        pltpu.VMEM((KVD, 2, rows2, HD), bf16),
        pltpu.VMEM((KVD, 2, tok, HD), bf16),
        pltpu.VMEM((length, rows), f32),
        pltpu.VMEM((length, rows), f32),
        pltpu.VMEM((length, rows), bf16),
        pltpu.VMEM((block, rows), bf16),
        pltpu.VMEM((HD, rows), f32),
        pltpu.VMEM((rows, HD), bf16),
        pltpu.VMEM((rows, HD), bf16),
        pltpu.VMEM((4, 8, rows), f32),
        pltpu.VMEM((8, rows), jnp.int32),
        pltpu.VMEM((2, 2, length, HD), f32),
        pltpu.VMEM((KVD, steps, 2, pair, HD), bf16),
        pltpu.VMEM((KVD, steps, 2, pair, HD), bf16),
        pltpu.VMEM((KVD, rows2, HD), bf16),
        pltpu.VMEM((KVD, rows2, HD), bf16),
        pltpu.VMEM((KVD, 2, tok, HD), bf16),
        pltpu.VMEM((KVD, 2, tok, HD), bf16),
        pltpu.VMEM((rounds + 1, 8, 128), f32),
        pltpu.VMEM((rounds, 8, 128), f32),
        dma((4, KVD)), dma((4, KVD)),
        dma((KVD, steps)), dma((KVD, steps)),
        dma((KVD, steps)), dma((KVD, steps)),
        dma((rounds,)), dma((rounds,)),
    ]
    return kernel, scratch


def body(queries, keys, values, out_grad, loss_mask):
    tok = queries.shape[1]
    ways = lax.axis_size("tensor")
    dp_size = lax.axis_size("dp")
    block = 256 if ways * tok % 256 == 0 else 2 * tok
    kernel, scratch = make_kernel(tok, dp_size, ways, block)
    vmem = pl.BlockSpec(memory_space=pltpu.VMEM)
    wide = jax.ShapeDtypeStruct((tok, queries.shape[2]), bf16)
    narrow = jax.ShapeDtypeStruct((tok, keys.shape[2]), bf16)
    query_grad, key_grad, value_grad = pl.pallas_call(
        kernel,
        out_shape=(wide, narrow, narrow),
        in_specs=[vmem] * 5,
        out_specs=(vmem, vmem, vmem),
        scratch_shapes=scratch,
        compiler_params=pltpu.CompilerParams(
            collective_id=0, has_side_effects=True, vmem_limit_bytes=62 * 2**20
        ),
    )(queries[0], keys[0], values[0], out_grad[0], loss_mask)
    return (query_grad[None], key_grad[None], value_grad[None])


def solution(mesh):
    return jax.shard_map(
        body,
        mesh=mesh,
        in_specs=(
            P("dp", "tensor", None),
            P("dp", "tensor", None),
            P("dp", "tensor", None),
            P("dp", "tensor", None),
            P("dp", "tensor"),
        ),
        out_specs=(P("dp", "tensor", None), P("dp", "tensor", None), P("dp", "tensor", None)),
        check_vma=False,
    )
```

time: 412 us -> 156 us (0.38)
  the two profiles are of different devices: /device:TPU:24 before, /device:TPU:16 now
where the time goes in v1:
time: 156 us
  Pallas kernels  151 us (97%)
  local copies, waits for them, and re-layouts  3.96 us (3%)
    pallas_call x1, Pallas kernels, body(): pl.pallas_call(kernel, out_shape=(wide, narrow, narrow), in_specs=[vmem]...  151 us
    unnamed x7, local copies, waits for them, and re-layouts  3.96 us

profile of v1, /device:TPU:16, one launch (start us, length us, event | category | flops | bytes accessed | tf_op | source)
XLA Modules:
  0.0 155.5 jit_solution(17151571378805367666)
XLA Ops:
  0.6 150.9 %shard_map.76 = (bf16[112,6144]{1,0:T(8,128)(2,1)}, bf16[112,1024]{1,0:T(8,128)(2,1)}, bf16[112,1024]{1,0:T(8,128)(2,1)}) custom-call(bf16[112,6144]{1,0:T(8,128)(2,1)} %bitcast.7, bf16[112,1024]{1,0:T(8,128)(2,1)} %bitcast.12, bf16[112,1024]{1,0:T(8,128)(2,1)} %bitcast.13, bf16[112,6144]{1,0:T(8,128)(2,1)} %bitcast.8, s32[1,112]{1,0:T(1,128)} %mask_ref.1), custom_call_target="tpu_custom_call" | custom-call | tf_op jit(solution)/shard_map/pallas_call | solution.py:468
  151.6 0.0 copy-start.1
  151.6 0.0 copy-start
  151.6 2.6 %copy.11 = bf16[1,112,6144]{2,1,0:T(8,128)(2,1)} copy(bf16[1,112,6144]{2,1,0:T(8,128)(2,1)} %bitcast.9) | data formatting | bytes 2752512
  154.2 0.0 copy-done.1
  154.2 0.7 copy.12
  154.9 0.0 copy-done
  154.9 0.7 copy.13
Async XLA Ops:
  151.6 2.6 %copy-start.1 = (bf16[112,1024]{1,0:T(8,128)(2,1)S(1)}, bf16[112,1024]{1,0:T(8,128)(2,1)}, u32[]{:S(2)}) copy-start(bf16[112,1024]{1,0:T(8,128)(2,1)} %get-tuple-element.7) | copy-start | bytes 688132
  151.6 3.3 %copy-start = (bf16[112,1024]{1,0:T(8,128)(2,1)S(1)}, bf16[112,1024]{1,0:T(8,128)(2,1)}, u32[]{:S(2)}) copy-start(bf16[112,1024]{1,0:T(8,128)(2,1)} %get-tuple-element.8) | copy-start | bytes 688132

commit v2 on v1

v2 whole, which is shorter than its diff:
```python
import jax
import jax.numpy as jnp
from jax import lax
from jax.experimental import pallas as pl
from jax.experimental.pallas import tpu as pltpu
from jax.sharding import PartitionSpec as P

HD = 128
KVH = 8
GROUP = 6
KVD = KVH // 2
RING = 8
UP = 4
DOWN = 3
SCALE = HD**-0.5
SCALE2 = SCALE * 1.4426950408889634
NT = (((1,), (1,)), ((), ()))
PARTS = 3
MESH = pl.DeviceIdType.MESH
f32 = jnp.float32
bf16 = jnp.bfloat16


def fold8(x):
    return x.reshape(x.shape[0] // 8, 8, x.shape[1])


def make_kernel(tok, dp_size, ways, block):
    rows2 = GROUP * tok
    rows = 2 * rows2
    pair = 2 * tok
    length = ways * tok
    blocks = length // block
    chunks = [(i, min(256, rows - i)) for i in range(0, rows, 256)]

    def digits(size):
        found, low = [], 1
        while low < size:
            found.append((low, min(4, size // low)))
            low *= found[-1][1]
        return found

    t_digits, dp_digits = digits(ways), digits(dp_size)

    def kernel(
        q_ref, k_ref, v_ref, g_ref, mask_ref, dq_ref, dk_ref, dv_ref,
        qg, kv, qg_out, kv_out, pbuf, ebuf, dsb, key_cols, dqt, qn, gn, stat, scales, rowpos,
        part, rs_out, rs_in, dq_out, dq_in, dkv_out, dkv_in, cnt_out, cnt_in,
        x_send, x_recv, ag_send, ag_recv, rs_send, rs_recv, cnt_send, cnt_recv,
    ):
        me_dp = lax.axis_index("dp")
        me = lax.axis_index("tensor")
        side = lax.rem(me, 2)
        y = me // 2

        def flips(index, low, size):
            digit = lax.rem(index // low, size)
            return [index + low * (lax.rem(digit + n, size) - digit) for n in range(1, size)]

        other = (me_dp, me + 1 - 2 * side)
        above = (me_dp, lax.rem(me + 2, ways))
        below = (me_dp, lax.rem(me + ways - 2, ways))
        rounds = [[(me_dp, t) for t in flips(me, low, size)] for low, size in t_digits] + [
            [(d, me) for d in flips(me_dp, low, size)] for low, size in dp_digits
        ]
        corner = me - lax.rem(me, 4) + 3 - lax.rem(me, 4)
        peers = [other, above, below, (me_dp, corner)]
        peers += [peer for group in rounds[1:] for peer in group]
        def clear(j, _):
            after = pl.ds(pl.multiple_of(j * pair, 16), pair)
            for h in range(KVD):
                kv[h, :, after, :] = jnp.zeros((2, pair, HD), bf16)
            return 0

        lax.fori_loop(y + 1, RING, clear, 0)
        barrier = pltpu.get_barrier_semaphore()
        for peer in peers:
            pl.semaphore_signal(barrier, inc=1, device_id=peer, device_id_type=MESH)

        def remote(src, dst, send, recv, device):
            return pltpu.make_async_remote_copy(
                src_ref=src, dst_ref=dst, send_sem=send, recv_sem=recv,
                device_id=device, device_id_type=MESH,
            )

        mask_row = mask_ref[...].astype(f32)
        eye = lax.broadcasted_iota(jnp.int32, (tok, tok), 0) == lax.broadcasted_iota(
            jnp.int32, (tok, tok), 1
        )
        mask_col = jnp.sum(jnp.where(eye, mask_row, 0.0), axis=1, keepdims=True)
        mask_tile = jnp.broadcast_to(mask_col, (tok, HD)).astype(bf16)
        cnt_out[0] = jnp.full((8, 128), jnp.sum(mask_row, keepdims=True)[0:1, 0:1], f32)

        own_rows = pl.multiple_of(side * rows2, 16)
        own_tok = pl.multiple_of(y * pair + side * tok, 16)

        def stage(h, _):
            for p in range(GROUP):
                at = pl.ds(p * tok, tok)
                mine = pl.ds(pl.multiple_of(((side * KVD + h) * GROUP + p) * HD, HD), HD)
                theirs = pl.ds(pl.multiple_of((((1 - side) * KVD + h) * GROUP + p) * HD, HD), HD)
                keep = pl.ds(pl.multiple_of(own_rows + p * tok, 16), tok)
                qg[h, 0, keep, :] = q_ref[:, mine]
                qg[h, 1, keep, :] = g_ref[:, mine] * mask_tile
                qg_out[h, 0, at, :] = q_ref[:, theirs]
                qg_out[h, 1, at, :] = g_ref[:, theirs] * mask_tile
            mine = pl.ds(pl.multiple_of((side * KVD + h) * HD, HD), HD)
            theirs = pl.ds(pl.multiple_of(((1 - side) * KVD + h) * HD, HD), HD)
            kv[h, 0, pl.ds(own_tok, tok), :] = k_ref[:, mine]
            kv[h, 1, pl.ds(own_tok, tok), :] = v_ref[:, mine]
            kv_out[h, 0] = k_ref[:, theirs]
            kv_out[h, 1] = v_ref[:, theirs]
            return 0

        lax.fori_loop(0, KVD, stage, 0)

        def clear_ds(b, _):
            dsb[pl.ds(pl.multiple_of(b * block, 16), block), :] = jnp.zeros((block, rows), bf16)
            return 0

        lax.fori_loop(0, blocks, clear_ds, 0)
        index = lax.broadcasted_iota(jnp.int32, (8, rows), 1)
        place = index
        for step in range(1, 2 * GROUP):
            place = place - jnp.where(index >= step * tok, tok, 0)
        rowpos[...] = place + jnp.where(index >= rows2, tok, 0)

        pl.semaphore_wait(barrier, len(peers))

        def x_copy(kind, h):
            src, dst = {
                0: lambda: (kv_out.at[h], kv.at[h, :, pl.ds(own_tok, tok), :]),
                1: lambda: (qg_out.at[h], qg.at[h, :, pl.ds(own_rows, rows2), :]),
                2: lambda: (dq_out.at[h], dq_in.at[h]),
                3: lambda: (dkv_out.at[h], dkv_in.at[h]),
            }[kind]()
            return remote(src, dst, x_send.at[kind, h], x_recv.at[kind, h], other)

        def ag_copy(h, s, up, i):
            j = y - s if up else lax.rem(y + s, RING)
            span = pl.ds(pl.multiple_of(jnp.maximum(j, 0) * pair, 16), pair)
            place = kv.at[h, i, span, :]
            slot = s if up else UP + s
            return remote(
                place, place, ag_send.at[h, slot, i], ag_recv.at[h, slot, i],
                above if up else below,
            )

        def ag_send_when(s, up):
            if up:
                return jnp.logical_and(y < RING - 1, y >= s)
            return lax.rem(y + s, RING) < DOWN

        def ag_recv_when(s, up):
            if up:
                return y >= s + 1
            return lax.rem(y + 1 + s, RING) < DOWN

        def ag_event(h, s):
            if s == 0:
                x_copy(0, h).wait_recv()
            for i in range(2):
                for up in (True, False):
                    last = UP if up else DOWN
                    if 1 <= s <= last:
                        pl.when(ag_recv_when(s - 1, up))(
                            lambda up=up, i=i: ag_copy(h, s - 1, up, i).wait_recv()
                        )
                    if s < last:
                        pl.when(ag_send_when(s, up))(
                            lambda up=up, i=i: ag_copy(h, s, up, i).start()
                        )

        def rs_copy(h, s, down):
            slot = s if down else UP + s
            return remote(
                rs_out.at[h, slot], rs_in.at[h, slot], rs_send.at[h, slot], rs_recv.at[h, slot],
                below if down else above,
            )

        def rs_block(s, down):
            return y - UP + s if down else lax.rem(y + DOWN - s, RING)

        def rs_send_when(s, down):
            if down:
                return y >= UP - s
            return lax.rem(y + DOWN - s, RING) < DOWN

        def rs_recv_when(s, down):
            if down:
                return jnp.logical_and(y < RING - 1, y >= UP - 1 - s)
            return lax.rem(y + DOWN - 1 - s, RING) < DOWN

        def rs_take(h, s, down):
            pl.when(rs_recv_when(s, down))(lambda: rs_copy(h, s, down).wait_recv())

        def the_factor():
            return f32(dp_size * length) / cnt_out[len(rounds)][0:1, :]

        def part_block(h, i, j):
            span = pl.ds(pl.multiple_of(jnp.maximum(j, 0) * pair, 16), pair)
            return part[lax.rem(h, PARTS), i, span, :]

        def rs_start(h, s):
            for down in (True, False):
                if s >= (UP if down else DOWN):
                    continue
                if s > 0:
                    rs_take(h, s - 1, down)
                slot = s if down else UP + s
                j = rs_block(s, down)
                here = rs_send_when(s, down)
                if down:
                    cases = [(True, s > 0, jnp.logical_and(here, y < RING - 1))]
                else:
                    cases = [(True, s > 0, jnp.logical_and(here, y > j))]
                    if s > 0:
                        cases.append((False, True, jnp.logical_and(here, y <= j)))
                for mine, came, when in cases:

                    def fill(mine=mine, came=came, slot=slot, j=j, down=down):
                        for i in range(2):
                            if mine and came:
                                total = part_block(h, i, j) + rs_in[h, slot - 1, i].astype(f32)
                                rs_out[h, slot, i] = total.astype(bf16)
                            elif mine:
                                rs_out[h, slot, i] = part_block(h, i, j).astype(bf16)
                            else:
                                rs_out[h, slot, i] = rs_in[h, slot - 1, i]
                        rs_copy(h, s, down).start()

                    pl.when(when)(fill)

        def rs_end(h, s):
            @pl.when(y == RING - 1)
            def _():
                for i in range(2):
                    rs_out[h, s, i] = part_block(h, i, RING - 1 - UP + s).astype(bf16)
                rs_copy(h, s, True).start()

        def rs_finish(h):
            rs_take(h, UP - 1, True)
            rs_take(h, DOWN - 1, False)
            mine_at = pl.ds(own_tok, tok)
            theirs_at = pl.ds(pl.multiple_of(y * pair + (1 - side) * tok, 16), tok)
            mine_in = pl.ds(pl.multiple_of(side * tok, 16), tok)
            theirs_in = pl.ds(pl.multiple_of((1 - side) * tok, 16), tok)
            columns = pl.ds(pl.multiple_of((side * KVD + h) * HD, HD), HD)
            from_above = y < RING - 1
            from_below = y < DOWN

            def total(i, at, within, above_too, below_too):
                value = part[lax.rem(h, PARTS), i, at, :]
                if above_too:
                    value = value + rs_in[h, UP - 1, i, within, :].astype(f32)
                if below_too:
                    value = value + rs_in[h, UP + DOWN - 1, i, within, :].astype(f32)
                return (value * (the_factor() * (SCALE if i == 0 else 1.0))).astype(bf16)

            for above_too, below_too, when in (
                (True, True, from_below),
                (True, False, jnp.logical_and(from_above, jnp.logical_not(from_below))),
                (False, False, jnp.logical_not(from_above)),
            ):

                def fill(above_too=above_too, below_too=below_too):
                    for i, ref in ((0, dk_ref), (1, dv_ref)):
                        dkv_out[h, i] = total(i, theirs_at, theirs_in, above_too, below_too)
                        ref[:, columns] = total(i, mine_at, mine_in, above_too, below_too)

                pl.when(when)(fill)
            x_copy(3, h).start()

        def count_copies(n):
            return [
                remote(
                    cnt_out.at[n], cnt_in.at[n, i], cnt_send.at[n, i], cnt_recv.at[n, i], peer
                )
                for i, peer in enumerate(rounds[n])
            ]

        def count_point(n):
            if 0 < n <= len(rounds):
                total = cnt_out[n - 1]
                for i, copy in enumerate(count_copies(n - 1)):
                    copy.wait_recv()
                    total = total + cnt_in[n - 1, i]
                cnt_out[n] = total
            if n < len(rounds):
                for copy in count_copies(n):
                    copy.start()

        x_copy(0, 0).start()
        count_point(0)
        x_copy(1, 0).start()
        ag_event(0, 0)
        x_copy(0, 1).start()

        gathers = {
            (0, "A0"): [(0, 1)],
            (0, "A1"): [(0, 2)],
            (0, "A2"): [(0, 3), (1, 0)],
            (0, "A3"): [(0, 4)],
            (0, "C"): [(1, 1)],
            (0, "E"): [(1, 2), (2, 0)],
            (1, "A1"): [(1, 3)],
            (1, "A2"): [(2, 1)],
            (1, "A3"): [(1, 4)],
            (1, "C"): [(2, 2), (3, 0)],
            (1, "E"): [(2, 3), (3, 1)],
            (2, "A0"): [(2, 4)],
            (2, "A1"): [(3, 2)],
            (2, "C"): [(3, 3)],
            (2, "E"): [(3, 4)],
        }
        counts = {(0, "A0"): 1, (0, "A2"): 2, (0, "E"): 3, (1, "A0"): 4, (1, "A2"): 5}
        exchanges = {
            (0, "A1"): [(1, 1), (0, 2)],
            (0, "C"): [(1, 2), (0, 3)],
            (1, "A0"): [(1, 3)],
        }

        def beside(h, place):
            for n in range(KVD):
                todo = (n, place)
                if todo not in gathers and todo not in counts and todo not in exchanges:
                    continue

                @pl.when(h == n)
                def _():
                    for kind, head in exchanges.get(todo, []):
                        x_copy(kind, head).start()
                    for head, s in gathers.get(todo, []):
                        ag_event(head, s)
                    if todo in counts:
                        count_point(counts[todo])

            if place in ("A1", "A2", "A3"):
                pl.when(h > 0)(lambda: rs_end(h - 1, int(place[1])))
            if place == "A2":
                pl.when(h > 0)(lambda: rs_start(h - 1, 1))
                pl.when(h > 1)(lambda: rs_start(h - 2, 3))

        held = (pair * (y + 1) + block - 1) // block
        high = y // (RING - 2)
        odd = lax.rem(y, 2)
        tiles = [
            (held - 1, None),
            (high * (2 - 2 * odd), y >= RING - 2),
            (high * 2 * odd + (1 - high) * jnp.maximum(held - 2, 0), held >= 2),
            (high + (1 - high) * jnp.maximum(held - 3, 0), held >= 3),
        ]

        def finish_queries(h):
            dq_rows = jnp.transpose(dqt[...] * (the_factor()[:, 0:1] * SCALE)).astype(bf16)

            def hand_out(mine, theirs):
                dq_out[h] = theirs
                for p in range(GROUP):
                    column = pl.multiple_of(((side * KVD + h) * GROUP + p) * HD, HD)
                    dq_ref[:, pl.ds(column, HD)] = mine[p * tok : (p + 1) * tok]

            pl.when(side == 0)(lambda: hand_out(dq_rows[:rows2], dq_rows[rows2:]))
            pl.when(side == 1)(lambda: hand_out(dq_rows[rows2:], dq_rows[:rows2]))
            x_copy(2, h).start()

        def one_head(h, _):
            stat[0] = jnp.full((8, rows), -1e30, f32)
            stat[1] = jnp.zeros((8, rows), f32)
            stat[2] = jnp.zeros((8, rows), f32)
            def weights(masked):
                def step(b, _):
                    at = pl.ds(pl.multiple_of(b * block, 16), block)
                    key_block = kv[h, 0, at, :]
                    value_block = kv[h, 1, at, :]
                    for c0, cw in chunks:
                        cs = pl.ds(c0, cw)
                        s = lax.dot_general(
                            key_block, qg[h, 0, cs, :], NT, preferred_element_type=f32
                        )
                        p = lax.dot_general(
                            value_block, qg[h, 1, cs, :], NT, preferred_element_type=f32
                        )
                        s = s * SCALE2
                        if masked:
                            key_at = (
                                b * block - pair * y
                                + lax.broadcasted_iota(jnp.int32, (block, cw), 0)
                            )
                            s = jnp.where(key_at <= rowpos[0:1, cs], s, -1e30)
                        pbuf[at, cs] = p
                        top = jnp.max(jnp.max(fold8(s), axis=0), axis=0, keepdims=True)
                        old = stat[0, 0:1, cs]
                        new = jnp.maximum(old, jnp.ceil(top))
                        change = jnp.exp2(old - new)
                        e = jnp.exp2(s - new)
                        ebuf[at, cs] = e.astype(bf16)
                        stat[0, :, cs] = jnp.broadcast_to(new, (8, cw))
                        scales[b, :, cs] = jnp.broadcast_to(new, (8, cw))
                        stat[1, :, cs] = stat[1, :, cs] * change + jnp.sum(fold8(e), axis=0)
                        stat[2, :, cs] = stat[2, :, cs] * change + jnp.sum(fold8(e * p), axis=0)
                    return 0

                return step

            beside(h, "A0")
            x_copy(1, h).wait_recv()
            for n, (tile, when) in enumerate(tiles):
                if n == 0:
                    weights(True)(tile, 0)
                else:
                    beside(h, f"A{n}")
                    pl.when(when)(lambda tile=tile: (weights(False)(tile, 0), None)[1])
            beside(h, "C")
            pl.when(h > 0)(lambda: finish_queries(h - 1))
            key_cols[...] = jnp.transpose(kv[h, 0])
            inverse = 1.0 / jnp.sum(stat[1], axis=0, keepdims=True)
            delta = jnp.sum(stat[2], axis=0, keepdims=True) * inverse
            stat[3] = jnp.broadcast_to(delta, (8, rows))
            inverse_column = jnp.transpose(jnp.broadcast_to(inverse, (8, rows)))[:, 0:1]
            qn[...] = (qg[h, 0].astype(f32) * inverse_column).astype(bf16)
            gn[...] = (qg[h, 1].astype(f32) * inverse_column).astype(bf16)
            slot = lax.rem(h, PARTS)

            def grads(b, _):
                at = pl.ds(pl.multiple_of(b * block, 16), block)
                for c0, cw in chunks:
                    cs = pl.ds(c0, cw)
                    change = jnp.exp2(scales[b, 0:1, cs] - stat[0, 0:1, cs]).astype(bf16)
                    e = ebuf[at, cs] * change
                    ebuf[at, cs] = e
                    dsb[at, cs] = e * (pbuf[at, cs] - stat[3, 0:1, cs]).astype(bf16)
                part[slot, 1, at, :] = jnp.dot(
                    ebuf[at, :], gn[...], preferred_element_type=f32
                )
                part[slot, 0, at, :] = jnp.dot(
                    dsb[at, :], qn[...], preferred_element_type=f32
                )
                return 0

            lax.fori_loop(0, held, grads, 0)
            rs_end(h, 0)
            rs_start(h, 0)
            beside(h, "E")
            for c0, cw in chunks:
                cs = pl.ds(c0, cw)
                dqt[:, cs] = inverse[:, c0 : c0 + cw] * jnp.dot(
                    key_cols[...], dsb[:, cs], preferred_element_type=f32
                )
            pl.when(h > 0)(lambda: rs_start(h - 1, 2))
            pl.when(h > 1)(lambda: rs_finish(h - 2))
            return 0

        lax.fori_loop(0, KVD, one_head, 0)
        last = KVD - 1

        @pl.when(y == RING - 1)
        def _():
            for s in range(1, UP):
                rs_copy(last, s - 1, True).wait_send()
                rs_end(last, s)

        finish_queries(last)

        def take_queries(h):
            x_copy(2, h).wait_recv()
            for p in range(GROUP):
                column = pl.multiple_of((((1 - side) * KVD + h) * GROUP + p) * HD, HD)
                dq_ref[:, pl.ds(column, HD)] = dq_in[h, p * tok : (p + 1) * tok, :]

        def settle(h, _):
            pl.when(h < last)(lambda: take_queries(h))
            for kind in range(3):
                x_copy(kind, h).wait_send()
            for s in range(UP):
                for way in (True, False):
                    if s < (UP if way else DOWN):
                        for i in range(2):
                            pl.when(ag_send_when(s, way))(
                                lambda s=s, way=way, i=i: ag_copy(h, s, way, i).wait_send()
                            )
            return 0

        def settle_sums(h, _):
            for s in range(UP):
                for way in (True, False):
                    if s < (UP if way else DOWN):
                        left = rs_send_when(s, way)
                        if way and s < UP - 1:
                            left = jnp.logical_and(left, jnp.logical_or(y < RING - 1, h < last))
                        pl.when(left)(lambda s=s, way=way: rs_copy(h, s, way).wait_send())
            return 0

        def take_sums(h, _):
            x_copy(3, h).wait_recv()
            columns = pl.ds(pl.multiple_of(((1 - side) * KVD + h) * HD, HD), HD)
            dk_ref[:, columns] = dkv_in[h, 0]
            dv_ref[:, columns] = dkv_in[h, 1]
            x_copy(3, h).wait_send()
            return 0

        rs_start(last, 1)
        rs_start(last - 1, 3)
        lax.fori_loop(0, KVD, settle, 0)
        rs_start(last, 2)
        rs_finish(last - 1)
        lax.fori_loop(0, last, settle_sums, 0)
        rs_start(last, 3)
        take_queries(last)
        lax.fori_loop(0, last, take_sums, 0)
        rs_finish(last)
        settle_sums(last, 0)
        take_sums(last, 0)
        for n in range(len(rounds)):
            for copy in count_copies(n):
                copy.wait_send()

    steps = UP + DOWN
    rounds = len(t_digits) + len(dp_digits)
    dma = pltpu.SemaphoreType.DMA
    scratch = [
        pltpu.VMEM((KVD, 2, rows, HD), bf16),
        pltpu.VMEM((KVD, 2, length, HD), bf16),
        pltpu.VMEM((KVD, 2, rows2, HD), bf16),
        pltpu.VMEM((KVD, 2, tok, HD), bf16),
        pltpu.VMEM((length, rows), f32),
        pltpu.VMEM((length, rows), bf16),
        pltpu.VMEM((length, rows), bf16),
        pltpu.VMEM((HD, length), bf16),
        pltpu.VMEM((HD, rows), f32),
        pltpu.VMEM((rows, HD), bf16),
        pltpu.VMEM((rows, HD), bf16),
        pltpu.VMEM((4, 8, rows), f32),
        pltpu.VMEM((blocks, 8, rows), f32),
        pltpu.VMEM((8, rows), jnp.int32),
        pltpu.VMEM((PARTS, 2, length, HD), f32),
        pltpu.VMEM((KVD, steps, 2, pair, HD), bf16),
        pltpu.VMEM((KVD, steps, 2, pair, HD), bf16),
        pltpu.VMEM((KVD, rows2, HD), bf16),
        pltpu.VMEM((KVD, rows2, HD), bf16),
        pltpu.VMEM((KVD, 2, tok, HD), bf16),
        pltpu.VMEM((KVD, 2, tok, HD), bf16),
        pltpu.VMEM((rounds + 1, 8, 128), f32),
        pltpu.VMEM((rounds, 3, 8, 128), f32),
        dma((4, KVD)), dma((4, KVD)),
        dma((KVD, steps, 2)), dma((KVD, steps, 2)),
        dma((KVD, steps)), dma((KVD, steps)),
        dma((rounds, 3)), dma((rounds, 3)),
    ]
    return kernel, scratch


def body(queries, keys, values, out_grad, loss_mask):
    tok = queries.shape[1]
    ways = lax.axis_size("tensor")
    dp_size = lax.axis_size("dp")
    block = 4 * tok
    kernel, scratch = make_kernel(tok, dp_size, ways, block)
    vmem = pl.BlockSpec(memory_space=pltpu.VMEM)
    wide = jax.ShapeDtypeStruct((tok, queries.shape[2]), bf16)
    narrow = jax.ShapeDtypeStruct((tok, keys.shape[2]), bf16)
    query_grad, key_grad, value_grad = pl.pallas_call(
        kernel,
        out_shape=(wide, narrow, narrow),
        in_specs=[vmem] * 5,
        out_specs=(vmem, vmem, vmem),
        scratch_shapes=scratch,
        compiler_params=pltpu.CompilerParams(
            collective_id=0, has_side_effects=True, vmem_limit_bytes=62 * 2**20
        ),
    )(queries[0], keys[0], values[0], out_grad[0], loss_mask)
    return (query_grad[None], key_grad[None], value_grad[None])


def solution(mesh):
    return jax.shard_map(
        body,
        mesh=mesh,
        in_specs=(
            P("dp", "tensor", None),
            P("dp", "tensor", None),
            P("dp", "tensor", None),
            P("dp", "tensor", None),
            P("dp", "tensor"),
        ),
        out_specs=(P("dp", "tensor", None), P("dp", "tensor", None), P("dp", "tensor", None)),
        check_vma=False,
    )
```

time: 156 us -> 120 us (0.77)
  the two profiles are of different devices: /device:TPU:16 before, /device:TPU:20 now
where the time goes in v2:
time: 120 us; the launch traced here: 119 us
  Pallas kernels  115 us (96%)
  local copies, waits for them, and re-layouts  3.96 us (3%)
    pallas_call x1, Pallas kernels, body(): pl.pallas_call(kernel, out_shape=(wide, narrow, narrow), in_specs=[vmem]...  115 us
    unnamed x7, local copies, waits for them, and re-layouts  3.96 us

profile of v2, /device:TPU:20, one launch (start us, length us, event | category | flops | bytes accessed | tf_op | source)
XLA Modules:
  0.0 119.5 jit_solution(15533401508878005736)
XLA Ops:
  0.6 114.9 %shard_map.76 = (bf16[112,6144]{1,0:T(8,128)(2,1)}, bf16[112,1024]{1,0:T(8,128)(2,1)}, bf16[112,1024]{1,0:T(8,128)(2,1)}) custom-call(bf16[112,6144]{1,0:T(8,128)(2,1)} %bitcast.7, bf16[112,1024]{1,0:T(8,128)(2,1)} %bitcast.12, bf16[112,1024]{1,0:T(8,128)(2,1)} %bitcast.13, bf16[112,6144]{1,0:T(8,128)(2,1)} %bitcast.8, s32[1,112]{1,0:T(1,128)} %mask_ref.1), custom_call_target="tpu_custom_call" | custom-call | tf_op jit(solution)/shard_map/pallas_call | solution.py:562
  115.5 0.0 copy-start.1
  115.5 0.0 copy-start
  115.5 2.6 %copy.11 = bf16[1,112,6144]{2,1,0:T(8,128)(2,1)} copy(bf16[1,112,6144]{2,1,0:T(8,128)(2,1)} %bitcast.9) | data formatting | bytes 2752512
  118.1 0.0 copy-done.1
  118.1 0.7 copy.12
  118.8 0.0 copy-done
  118.8 0.7 copy.13
Async XLA Ops:
  115.5 2.6 %copy-start.1 = (bf16[112,1024]{1,0:T(8,128)(2,1)S(1)}, bf16[112,1024]{1,0:T(8,128)(2,1)}, u32[]{:S(2)}) copy-start(bf16[112,1024]{1,0:T(8,128)(2,1)} %get-tuple-element.7) | copy-start | bytes 688132
  115.5 3.3 %copy-start = (bf16[112,1024]{1,0:T(8,128)(2,1)S(1)}, bf16[112,1024]{1,0:T(8,128)(2,1)}, u32[]{:S(2)}) copy-start(bf16[112,1024]{1,0:T(8,128)(2,1)} %get-tuple-element.8) | copy-start | bytes 688132

commit v3 on v2

--- a/solution.py
+++ b/solution.py
@@ -292,8 +292,8 @@
 
         x_copy(0, 0).start()
         count_point(0)
+        ag_event(0, 0)
         x_copy(1, 0).start()
-        ag_event(0, 0)
         x_copy(0, 1).start()
 
         gathers = {
@@ -352,7 +352,7 @@
         ]
 
         def finish_queries(h):
-            dq_rows = jnp.transpose(dqt[...] * (the_factor()[:, 0:1] * SCALE)).astype(bf16)
+            dq_rows = jnp.transpose((dqt[...] * (the_factor()[:, 0:1] * SCALE)).astype(bf16))
 
             def hand_out(mine, theirs):
                 dq_out[h] = theirs

time: 120 us -> 121 us (level)
  the two profiles are of different devices: /device:TPU:20 before, /device:TPU:16 now
where the time goes in v3:
time: 121 us
  Pallas kernels  116 us (96%)
  local copies, waits for them, and re-layouts  3.96 us (3%)
    pallas_call x1, Pallas kernels, body(): pl.pallas_call(kernel, out_shape=(wide, narrow, narrow), in_specs=[vmem]...  116 us
    unnamed x7, local copies, waits for them, and re-layouts  3.96 us

profile of v3, /device:TPU:16, one launch (start us, length us, event | category | flops | bytes accessed | tf_op | source)
XLA Modules:
  0.0 121.0 jit_solution(14585546428243355684)
XLA Ops:
  0.6 116.4 %shard_map.76 = (bf16[112,6144]{1,0:T(8,128)(2,1)}, bf16[112,1024]{1,0:T(8,128)(2,1)}, bf16[112,1024]{1,0:T(8,128)(2,1)}) custom-call(bf16[112,6144]{1,0:T(8,128)(2,1)} %bitcast.7, bf16[112,1024]{1,0:T(8,128)(2,1)} %bitcast.12, bf16[112,1024]{1,0:T(8,128)(2,1)} %bitcast.13, bf16[112,6144]{1,0:T(8,128)(2,1)} %bitcast.8, s32[1,112]{1,0:T(1,128)} %mask_ref.1), custom_call_target="tpu_custom_call" | custom-call | tf_op jit(solution)/shard_map/pallas_call | solution.py:562
  117.0 0.0 copy-start.1
  117.0 0.0 copy-start
  117.0 2.6 %copy.11 = bf16[1,112,6144]{2,1,0:T(8,128)(2,1)} copy(bf16[1,112,6144]{2,1,0:T(8,128)(2,1)} %bitcast.9) | data formatting | bytes 2752512
  119.6 0.0 copy-done.1
  119.6 0.7 copy.12
  120.3 0.0 copy-done
  120.3 0.7 copy.13
Async XLA Ops:
  117.0 2.6 %copy-start.1 = (bf16[112,1024]{1,0:T(8,128)(2,1)S(1)}, bf16[112,1024]{1,0:T(8,128)(2,1)}, u32[]{:S(2)}) copy-start(bf16[112,1024]{1,0:T(8,128)(2,1)} %get-tuple-element.7) | copy-start | bytes 688132
  117.0 3.3 %copy-start = (bf16[112,1024]{1,0:T(8,128)(2,1)S(1)}, bf16[112,1024]{1,0:T(8,128)(2,1)}, u32[]{:S(2)}) copy-start(bf16[112,1024]{1,0:T(8,128)(2,1)} %get-tuple-element.8) | copy-start | bytes 688132
